TPU v7x, 512 devices: a whole 4x8x8 slice. The times are simulated.
512 devices in a mesh: dp: 32 (over z, x_hi, core), comp: 16 (over x_lo, y).
Axes of the slice: x: 4 (x_hi: 2, x_lo: 2; x = x_hi * 2 + x_lo), y: 8, z: 8, core: 2. Of those that a mesh axis runs over, the one named last changes fastest.
Arguments:
- embeddings: float32 [32768, 768], P('dp'), may hold values from -6 to 6
- comp_means: float32 [8192, 768], P(('comp', 'dp')), may hold values from -1.2 to 1.2
- comp_variances: float32 [8192, 768], P(('comp', 'dp')), may hold values from 0.8 to 1.25
- comp_mass: float32 [8192], P(('comp', 'dp')), may hold values from 0.3 to 3
Outputs:
- new_means: float32 [8192, 768], P(('comp', 'dp'))
- new_variances: float32 [8192, 768], P(('comp', 'dp'))
- new_mass: float32 [8192], P(('comp', 'dp'))
All inputs are finite; a program needn't handle non-finite values.
Results may differ from a plain program's by a relative error of at most 0.0003.
Values sent between devices are 32-bit elements; how exact they have to be, the bound alone decides.
A program may use at most 64 MiB of HBM per device.

v0:
```python
import jax
import jax.numpy as jnp
from jax import lax
from jax.sharding import PartitionSpec as P


def coefficients(comp_means, comp_variances, comp_mass):
    precision = 1.0 / comp_variances
    neg_half = -0.5 * precision
    mean_prec = comp_means * precision
    offset = jnp.log(comp_mass) - 0.5 * jnp.sum(
        jnp.log(comp_variances) + comp_means * mean_prec, axis=1
    )
    return (neg_half, mean_prec, offset)


def moments_of(responsibility, values):
    return lax.dot_general(
        responsibility,
        values,
        (((0,), (0,)), ((), ())),
        precision=lax.Precision.HIGHEST,
        preferred_element_type=jnp.float32,
    )


def per_device(embeddings, comp_means, comp_variances, comp_mass):
    highest = lax.Precision.HIGHEST
    squares = embeddings * embeddings
    piece_half, piece_prec, piece_offset = coefficients(
        lax.all_gather(comp_means, "dp", axis=0, tiled=True),
        lax.all_gather(comp_variances, "dp", axis=0, tiled=True),
        lax.all_gather(comp_mass, "dp", axis=0, tiled=True),
    )
    quad = jnp.dot(squares, piece_half.T, precision=highest, preferred_element_type=jnp.float32)
    linear = jnp.dot(
        embeddings, piece_prec.T, precision=highest, preferred_element_type=jnp.float32
    )
    scores = quad + linear + piece_offset[None, :]
    local_peak = jnp.max(scores, axis=1)
    row_peak = lax.pmax(local_peak, "comp")
    shifted = jnp.exp(scores - row_peak[:, None])
    row_total = lax.psum(jnp.sum(shifted, axis=1), "comp")
    responsibility = shifted / row_total[:, None]
    first_sums = moments_of(responsibility, embeddings)
    second_sums = moments_of(responsibility, squares)
    counts = jnp.sum(responsibility, axis=0)
    first_sums, second_sums, counts = (
        lax.psum_scatter(first_sums, "dp", scatter_dimension=0, tiled=True),
        lax.psum_scatter(second_sums, "dp", scatter_dimension=0, tiled=True),
        lax.psum_scatter(counts, "dp", scatter_dimension=0, tiled=True),
    )
    total_comps = comp_means.shape[0] * lax.axis_size("dp") * lax.axis_size("comp")
    total_rows = embeddings.shape[0] * lax.axis_size("dp")
    mass_scale = total_comps / total_rows
    new_mass = 0.4 * comp_mass + 0.6 * mass_scale * counts
    first_moment = 0.4 * comp_mass[:, None] * comp_means + 0.6 * mass_scale * first_sums
    second_moment = (
        0.4 * comp_mass[:, None] * (comp_variances + comp_means * comp_means)
        + 0.6 * mass_scale * second_sums
    )
    new_means = first_moment / new_mass[:, None]
    new_variances = second_moment / new_mass[:, None] - new_means * new_means
    return (new_means, new_variances, new_mass)


def solution(mesh):
    placed = (P("dp", None), P(("comp", "dp"), None), P(("comp", "dp"), None), P(("comp", "dp")))
    return jax.shard_map(
        per_device,
        mesh=mesh,
        in_specs=placed,
        out_specs=(P(("comp", "dp"), None), P(("comp", "dp"), None), P(("comp", "dp"))),
        check_vma=False,
    )
```

profile of v0, /device:TPU:1, one launch (start us, length us, event | category | flops | bytes accessed | tf_op | source)
XLA Modules:
  0.0 525.9 jit_solution(17203534192863885605)
XLA Ops:
  7.2 0.0 all-gather.3.cloned.1.call-start
  7.2 0.7 all-gather.3.cloned.1.call-update
  7.9 0.0 all-gather.5.cloned.1.call-start
  7.9 0.7 all-gather.5.cloned.1.call-update
  8.6 0.0 reduce-scatter.3.cloned.1.call-start
  8.7 1.4 fusion.21
  10.7 0.9 dynamic-update-slice
  11.6 72.3 %all-reduce = f32[512]{0:T(512)S(1)} all-reduce(f32[512]{0:T(512)S(1)} %dynamic-update-slice), channel_id=1, replica_groups=mesh['dp'=32,'comp'=16] {'dp'}, use_global_device_ids=true, to_apply=%add | all-reduce | flops 512 | bytes 4096
  83.8 18.3 %all-gather.3.cloned.1.call-done = f32[512,768]{1,0:T(8,128)} async-done(((f32[16,768]{1,0:T(8,128)}), f32[512,768]{1,0:T(8,128)}) %all-gather.3.cloned.1.call-update) | async-done | bytes 1572880 | tf_op jit(solution)/shard_map/all_gather | solution.py:32
  102.2 84.3 %all-gather.5.cloned.1.call-done = f32[512,768]{1,0:T(8,128)} async-done(((f32[16,768]{1,0:T(8,128)}), f32[512,768]{1,0:T(8,128)}) %all-gather.5.cloned.1.call-update) | async-done | bytes 1572880 | tf_op jit(solution)/shard_map/all_gather | solution.py:31
  186.4 2.6 add_reduce_fusion
  189.0 0.0 copy-done
  189.0 0.0 copy-done.2
  189.0 0.0 copy-start.1
  189.0 0.0 copy-start.3
  189.1 7.3 %fusion.10 = f32[512,1024]{1,0:T(8,128)S(1)} fusion(f32[1024,768]{1,0:T(8,128)} %param.4, f32[512,768]{1,0:T(8,128)S(1)} %copy-done.2, f32[512,768]{1,0:T(8,128)S(1)} %copy-done), kind=kOutput, calls=%fused_computation.11 | convolution fusion | flops 4832624640 | bytes 8388608 | tf_op jit(solution)/shard_map/dot_general | solution.py:36
  196.3 0.0 copy-done.1
  196.4 5.4 %fusion.22 = (f32[1024]{0:T(1024)S(1)}, f32[1024,512]{0,1:T(8,128)S(1)}) fusion(f32[512]{0:T(512)S(1)} %multiply_subtract_fusion.1, f32[512,1024]{1,0:T(8,128)S(1)} %fusion.10, f32[512,768]{1,0:T(8,128)S(1)} %copy-done.1, f32[1024,768]{1,0:T(8,128)S(1)} %copy-done.3), kind=kOutput, calls=%fused_computation.27 | convolution fusion | flops 4834982912 | bytes 8919040 | tf_op jit(solution)/shard_map/dot_general | solution.py:35
  201.8 26.4 %pmax.7 = f32[1024]{0:T(1024)S(1)} all-reduce(f32[1024]{0:T(1024)S(1)} %get-tuple-element.9), channel_id=1, replica_groups=mesh['dp'=32,'comp'=16] {'comp'}, use_global_device_ids=true, to_apply=%region_2.0 | all-reduce | flops 1024 | bytes 8192 | tf_op jit(solution)/shard_map/pmax | solution.py:41
  228.2 0.3 fusion.6
  228.5 23.8 %psum.7 = f32[1024]{0:T(1024)S(1)} all-reduce(f32[1024]{0:T(1024)S(1)} %fusion.6), channel_id=1, replica_groups=mesh['dp'=32,'comp'=16] {'comp'}, use_global_device_ids=true, to_apply=%region_4.0 | all-reduce | flops 1024 | bytes 8192 | tf_op jit(solution)/shard_map/psum | solution.py:43
  252.4 8.4 %fusion.19 = f32[512,768]{1,0:T(8,128)} fusion(f32[1024,768]{1,0:T(8,128)} %param.4, f32[1024,512]{0,1:T(8,128)S(1)} %get-tuple-element.10, f32[1024]{0:T(1024)S(1)} %psum.7, f32[1024]{0:T(1024)S(1)} %pmax.7), kind=kOutput, calls=%fused_computation.25 | convolution fusion | flops 4832886784 | bytes 6823936 | tf_op jit(solution)/shard_map/dot_general | solution.py:18
  260.8 0.0 reduce-scatter.3.cloned.1.call-update
  260.8 0.0 reduce-scatter.5.cloned.1.call-start
  260.9 8.5 %fusion = f32[512,768]{1,0:T(8,128)} fusion(f32[1024,768]{1,0:T(8,128)} %param.4, f32[1024,512]{0,1:T(8,128)S(1)} %get-tuple-element.10, f32[1024]{0:T(1024)S(1)} %psum.7, f32[1024]{0:T(1024)S(1)} %pmax.7), kind=kOutput, calls=%fused_computation | convolution fusion | flops 4833673216 | bytes 6823936 | tf_op jit(solution)/shard_map/dot_general | solution.py:18
  269.3 0.0 reduce-scatter.5.cloned.1.call-update
  270.1 0.4 fusion.18
  270.5 78.6 %all-reduce.1 = f32[512]{0:T(512)S(1)} all-reduce(f32[512]{0:T(512)S(1)} %fusion.18), channel_id=3, replica_groups=mesh['dp'=32,'comp'=16] {'dp'}, use_global_device_ids=true, to_apply=%region_7.0.clone | all-reduce | flops 512 | bytes 4096
  349.1 0.1 broadcast_multiply_fusion
  349.2 40.1 %reduce-scatter.3.cloned.1.call-done = f32[16,768]{1,0:T(8,128)} async-done(((f32[512,768]{1,0:T(8,128)}), f32[16,768]{1,0:T(8,128)}) %reduce-scatter.3.cloned.1.call-update) | async-done | bytes 49168 | tf_op jit(solution)/shard_map/reduce_scatter | solution.py:49
  389.3 128.5 %reduce-scatter.5.cloned.1.call-done = f32[16,768]{1,0:T(8,128)} async-done(((f32[512,768]{1,0:T(8,128)}), f32[16,768]{1,0:T(8,128)}) %reduce-scatter.5.cloned.1.call-update) | async-done | bytes 49168 | tf_op jit(solution)/shard_map/reduce_scatter | solution.py:50
  517.8 1.5 multiply_subtract_fusion
  (13 shorter events, 0.0 us)
Async XLA Ops:
  7.2 95.0 %all-gather.3.cloned.1.call-start = ((), (), s32[]{:S(2)}) async-start(), calls=%async_computation.2 | async-start | bytes 1622016 | tf_op jit(solution)/shard_map/all_gather | solution.py:32
  7.9 178.5 %all-gather.5.cloned.1.call-start = ((), (), s32[]{:S(2)}) async-start(), calls=%async_computation.3 | async-start | bytes 1622016 | tf_op jit(solution)/shard_map/all_gather | solution.py:31
  8.6 380.6 %reduce-scatter.3.cloned.1.call-start = ((), (), s32[]{:S(2)}) async-start(), calls=%async_computation.4 | async-start | bytes 1622016 | tf_op jit(solution)/shard_map/reduce_scatter | solution.py:49
  102.2 86.9 %copy-start = (f32[512,768]{1,0:T(8,128)S(1)}, f32[512,768]{1,0:T(8,128)}, u32[]{:S(2)}) copy-start(f32[512,768]{1,0:T(8,128)} %all-gather.3.cloned.1.call-done) | copy-start | bytes 4718596
  186.4 2.6 copy-start.2
  189.0 7.3 %copy-start.1 = (f32[512,768]{1,0:T(8,128)S(1)}, f32[512,768]{1,0:T(8,128)}, u32[]{:S(2)}) copy-start(f32[512,768]{1,0:T(8,128)} %all-gather.3.cloned.1.call-done) | copy-start | bytes 4718596
  189.0 7.3 %copy-start.3 = (f32[1024,768]{1,0:T(8,128)S(1)}, f32[1024,768]{1,0:T(8,128)}, u32[]{:S(2)}) copy-start(f32[1024,768]{1,0:T(8,128)} %param.4) | copy-start | bytes 9437188
  260.8 257.0 %reduce-scatter.5.cloned.1.call-start = ((), (), s32[]{:S(2)}) async-start(), calls=%async_computation.5 | async-start | bytes 1622016 | tf_op jit(solution)/shard_map/reduce_scatter | solution.py:50
  269.3 79.8 %copy-start.7 = (f32[16]{0:T(128)S(1)}, f32[16]{0:T(128)}, u32[]{:S(2)}) copy-start(f32[16]{0:T(128)} %param.7) | copy-start | bytes 196
  269.3 248.4 %copy-start.4 = (f32[16,768]{1,0:T(8,128)S(1)}, f32[16,768]{1,0:T(8,128)}, u32[]{:S(2)}) copy-start(f32[16,768]{1,0:T(8,128)} %param.6) | copy-start | bytes 147460
  269.3 248.4 %copy-start.5 = (f32[16,768]{1,0:T(8,128)S(1)}, f32[16,768]{1,0:T(8,128)}, u32[]{:S(2)}) copy-start(f32[16,768]{1,0:T(8,128)} %param.5) | copy-start | bytes 147460
  349.2 170.1 %copy-start.6 = (f32[16]{0:T(128)}, f32[16]{0:T(128)S(1)}, u32[]{:S(2)}) copy-start(f32[16]{0:T(128)S(1)} %get-tuple-element.8) | copy-start | bytes 196
Sparse Core Ops, SparseCore 0:
  11.4 90.7 all-gather.2
  105.5 80.8 all-gather.4
  260.9 128.3 reduce-scatter.2
  393.8 123.9 reduce-scatter.4
where the time goes:
time: 530 us; the launch traced here: 526 us
  waiting for transfers between devices  273 us (52%)
  blocking collectives  201 us (38%)
  matrix products  29.6 us (6%)
  between operations  15.2 us (3%)
    unnamed x2, blocking collectives  151 us
    reduce_scatter x1, waiting for transfers between devices, per_device(): lax.psum_scatter(second_sums, 'dp', scatter_dimension=0, tiled=True)  128 us
    all_gather x1, waiting for transfers between devices, per_device(): lax.all_gather(comp_means, 'dp', axis=0, tiled=True)  84.3 us
    reduce_scatter x1, waiting for transfers between devices, per_device(): lax.psum_scatter(first_sums, 'dp', scatter_dimension=0, tiled=True)  40.1 us
    pmax x1, blocking collectives, per_device(): row_peak = lax.pmax(local_peak, 'comp')  26.4 us
    psum x1, blocking collectives, per_device(): row_total = lax.psum(jnp.sum(shifted, axis=1), 'comp')  23.8 us
    all_gather x1, waiting for transfers between devices, per_device(): lax.all_gather(comp_variances, 'dp', axis=0, tiled=True)  18.3 us
    dot_general x2, matrix products, moments_of(): lax.dot_general(responsibility, values, (((0,), (0,)), ((), ())), precisi...  16.9 us
  transfers between devices with their start and end apart: 4, of which 4 were waited for; matrix products, arithmetic and copies ran while one was open for 2% of the time, Pallas kernels for 0%

commit v1 on v0

v1 whole, which is shorter than its diff:
```python
import functools

import jax
import jax.numpy as jnp
from jax import lax
from jax.experimental import pallas as pl
from jax.experimental.pallas import tpu as pltpu
from jax.sharding import PartitionSpec as P

MESH = pl.DeviceIdType.MESH
NT = (((1,), (1,)), ((), ()))
NN = (((1,), (0,)), ((), ()))


def split(value):
    high = value.astype(jnp.bfloat16)
    return high, (value - high.astype(jnp.float32)).astype(jnp.bfloat16)


def kernel(
    n_z, n_comp, mass_scale,
    emb_hbm, mean_ref, var_ref, mass_ref,
    new_mean_ref, new_var_ref, new_mass_ref,
    emb, wbuf, lhs, offs, xx_hi, xx_lo, st, stats, fac, rt,
    mbuf, sbuf, rbuf, lbuf, xbuf,
    emb_sem, gs, gr, ss, sr, ms, mr,
):
    f32 = jnp.float32
    rows, width = emb.shape
    own = mean_ref.shape[0]
    chunk = 2 * own
    half = n_z * chunk
    tiles = rows // 128
    dp, comp = lax.axis_index("dp"), lax.axis_index("comp")
    z, xh, core = dp // 4, (dp // 2) % 2, dp % 2
    other_x, other_core = 1 - xh, 1 - core

    def at(zz, xx, cc):
        return (zz * 4 + xx * 2 + cc, comp)

    def z_off(k):
        return (z + k + n_z) % n_z

    right, left = at(z_off(1), xh, core), at(z_off(-1), xh, core)
    partner, sibling = at(z, other_x, core), at(z, xh, other_core)

    emb_copy = pltpu.make_async_copy(emb_hbm, emb, emb_sem)
    emb_copy.start()
    barrier = pltpu.get_barrier_semaphore()
    for target in (right, left, partner, sibling):
        pl.semaphore_signal(barrier, inc=1, device_id=target, device_id_type=MESH)

    def greet(t, carry):
        peer = (dp, (comp + t) % n_comp)
        pl.semaphore_signal(barrier, inc=1, device_id=peer, device_id_type=MESH)
        return carry

    lax.fori_loop(1, n_comp, greet, 0)

    means, variances = mean_ref[...], var_ref[...]
    precision = 1.0 / variances
    mean_prec = means * precision
    diagonal = lax.broadcasted_iota(jnp.int32, (own, own), 0) == lax.broadcasted_iota(
        jnp.int32, (own, own), 1
    )
    mass = jnp.sum(
        jnp.where(diagonal, jnp.broadcast_to(mass_ref[...], (own, own)), 0.0), axis=1, keepdims=True
    )
    offset = jnp.log(mass) - 0.5 * jnp.sum(
        jnp.log(variances) + means * mean_prec, axis=1, keepdims=True
    )

    def w_rows(cc, zz, xx):
        return pl.ds(pl.multiple_of(cc * half + zz * chunk + xx * own, own), own)

    mine = w_rows(core, z, xh)
    wbuf[mine, 0:width] = -0.5 * precision
    wbuf[mine, width : 2 * width] = mean_prec
    wbuf[mine, 2 * width :] = jnp.broadcast_to(offset, (own, 128))

    pl.semaphore_wait(barrier, 4 + n_comp - 1)

    cols = (xh, other_x)

    def gather_copy(index, zz, c, target):
        place = w_rows(core, zz, cols[c])
        return pltpu.make_async_remote_copy(
            src_ref=wbuf.at[place], dst_ref=wbuf.at[place],
            send_sem=gs.at[index], recv_sem=gr.at[index],
            device_id=target, device_id_type=MESH,
        )

    def r_index(step, c):
        return 1 + (step - 1) * 2 + c

    def l_index(step, c):
        return 8 + (step - 1) * 2 + (c if step < 4 else 0)

    def s_index(k, c):
        return 15 + (k % 8) * 2 + c

    sent = []

    def send(index, zz, c, target):
        copy = gather_copy(index, zz, c, target)
        copy.start()
        sent.append(copy)

    def arrived(index):
        gather_copy(index, z, 0, partner).wait_recv()

    def to_sibling(k, c):
        send(s_index(k, c), z_off(k), c, sibling)

    send(r_index(1, 0), z, 0, right)
    send(l_index(1, 0), z, 0, left)
    send(0, z, 0, partner)
    to_sibling(0, 0)

    emb_copy.wait()

    def prepare(i, carry):
        place = pl.ds(pl.multiple_of(i * 128, 128), 128)
        x = emb[place, :]
        hi, lo = split(x * x)
        xx_hi[place, 0:width] = hi
        xx_lo[place, 0:width] = lo
        hi, lo = split(x)
        xx_hi[place, width:] = hi
        xx_lo[place, width:] = lo
        return carry

    lax.fori_loop(0, tiles, prepare, 0)

    sizes = (2 * chunk, 4 * chunk, 4 * chunk, 4 * chunk, 2 * chunk)
    bases = (0, 2 * chunk, 6 * chunk, 10 * chunk, 14 * chunk)

    def places(k):
        shifts = (k,) if k in (0, 4) else (-k, k)
        return [(cc, z_off(s)) for cc in (core, other_core) for s in shifts]

    def stage(k):
        n, base = sizes[k], bases[k]
        for i, (cc, zz) in enumerate(places(k)):
            place = pl.ds(pl.multiple_of(cc * half + zz * chunk, chunk), chunk)
            hi, lo = split(wbuf[place, 0 : 2 * width])
            lhs[i * chunk : (i + 1) * chunk, :] = hi
            lhs[n + i * chunk : n + (i + 1) * chunk, :] = lo
            offs[base + i * chunk : base + (i + 1) * chunk, :] = wbuf[place, 2 * width :]

    block = 256

    def score(k):
        n, base = sizes[k], bases[k]

        def body(b, carry):
            place = pl.ds(pl.multiple_of(b * block, block), block)
            both = lax.dot_general(
                lhs[0 : 2 * n, :], xx_hi[place, :], NT, preferred_element_type=f32
            )
            low = lax.dot_general(lhs[0:n, :], xx_lo[place, :], NT, preferred_element_type=f32)
            off = offs[base : base + n, :]
            st[base : base + n, place] = both[:n] + both[n:] + low + jnp.concatenate([off, off], 1)
            return carry

        lax.fori_loop(0, rows // block, body, 0)

    def sibling_arrived(ks):
        for k in ks:
            for c in range(2):
                arrived(s_index(k, c))

    arrived(0)
    send(r_index(1, 1), z, 1, right)
    send(l_index(1, 1), z, 1, left)
    to_sibling(0, 1)
    for step in range(1, 4):
        for c in range(2):
            arrived(r_index(step, c))
            if step < 3 or c == 0:
                send(r_index(step + 1, c), z_off(-step), c, right)
            arrived(l_index(step, c))
            if step < 3 or c == 1:
                send(l_index(step + 1, c), z_off(step), c, left)
            to_sibling(-step, c)
            to_sibling(step, c)
            if c == 0:
                if step == 1:
                    sibling_arrived((0,))
                else:
                    sibling_arrived((1 - step, step - 1))
                stage(step - 1)
                score(step - 1)
    sibling_arrived((-3, 3))
    stage(3)
    score(3)
    arrived(r_index(4, 0))
    to_sibling(4, 0)
    arrived(l_index(4, 1))
    to_sibling(4, 1)
    sibling_arrived((4,))
    stage(4)
    score(4)

    for i in range(tiles):
        lanes = slice(i * 128, (i + 1) * 128)
        s = st[:, lanes]
        peak = jnp.max(s, axis=0, keepdims=True)
        e = jnp.exp(s - peak)
        st[:, lanes] = e
        stats[comp, i : i + 1, :] = peak
        stats[comp, tiles + i : tiles + i + 1, :] = jnp.sum(e, axis=0, keepdims=True)

    def stat_copy(t):
        return pltpu.make_async_remote_copy(
            src_ref=stats.at[comp], dst_ref=stats.at[comp],
            send_sem=ss.at[t], recv_sem=sr.at[t],
            device_id=(dp, (comp + t) % n_comp), device_id_type=MESH,
        )

    def stat_start(t, carry):
        stat_copy(t).start()
        return carry

    def stat_wait(t, carry):
        stat_copy(t).wait_recv()
        return carry

    lax.fori_loop(1, n_comp, stat_start, 0)
    lax.fori_loop(1, n_comp, stat_wait, 0)
    peaks, totals = stats[:, 0:tiles, :], stats[:, tiles:, :]
    peak = jnp.max(peaks, axis=0)
    total = jnp.sum(totals * jnp.exp(peaks - peak[None]), axis=0)
    fac[...] = jnp.exp(stats[comp, 0:tiles, :] - peak) / total

    counts = None
    for i in range(tiles):
        lanes = slice(i * 128, (i + 1) * 128)
        resp = st[:, lanes] * fac[i : i + 1, :]
        counts = resp if counts is None else counts + resp
        hi, lo = split(resp)
        for n, base in zip(sizes, bases):
            rt[2 * base : 2 * base + n, lanes] = hi[base : base + n]
            rt[2 * base + n : 2 * base + 2 * n, lanes] = lo[base : base + n]
    mbuf[:, 2 * width :] = counts

    def moments(k):
        n, base = sizes[k], bases[k]

        def body(b, carry):
            lanes = pl.ds(pl.multiple_of(b * block, block), block)
            both = lax.dot_general(
                rt[2 * base : 2 * base + 2 * n, :], xx_hi[:, lanes], NN, preferred_element_type=f32
            )
            low = lax.dot_general(
                rt[2 * base : 2 * base + n, :], xx_lo[:, lanes], NN, preferred_element_type=f32
            )
            mbuf[base : base + n, lanes] = both[:n] + both[n:] + low
            return carry

        lax.fori_loop(0, 2 * width // block, body, 0)

    def reduce_copy(index, src, dst, target):
        return pltpu.make_async_remote_copy(
            src_ref=src, dst_ref=dst, send_sem=ms.at[index], recv_sem=mr.at[index],
            device_id=target, device_id_type=MESH,
        )

    def push(index, src, dst, target):
        copy = reduce_copy(index, src, dst, target)
        copy.start()
        sent.append(copy)

    def with_sibling(k):
        n, base = sizes[k], bases[k]
        h = n // 2
        theirs = mbuf.at[base + h : base + n]
        push(k, theirs, sbuf.at[base // 2 : base // 2 + h], sibling)

    def add_sibling(k):
        n, base = sizes[k], bases[k]
        h = n // 2
        landed = sbuf.at[base // 2 : base // 2 + h]
        reduce_copy(k, landed, landed, sibling).wait_recv()
        mbuf[base : base + h, :] += landed[...]

    def m_rows(k, c):
        side = 1 if 0 < k < 4 else 0
        start = bases[abs(k)] + side * chunk + cols[c] * own
        return pl.ds(pl.multiple_of(start, own), own)

    def slot(step, c):
        return 2 * (step - 1) - (1 if step > 1 else 0) + (c if step > 1 else 0)

    def pass_on(step, c, toward, buf, first, target):
        k = toward * (5 - step) if step > 1 else 4
        index = slot(step, c)
        if step == 1 or (step == 2 and c != first):
            src = mbuf.at[m_rows(k, c)]
        else:
            before = buf.at[slot(step - 1, c)]
            reduce_copy(base_of[toward] + slot(step - 1, c), before, before, target).wait_recv()
            before[...] += mbuf[m_rows(k, c), :]
            src = before
        push(base_of[toward] + index, src, buf.at[index], target)

    base_of = {1: 5, -1: 12}
    moments(4)
    with_sibling(4)
    add_sibling(4)
    pass_on(1, 0, 1, rbuf, 0, right)
    pass_on(1, 1, -1, lbuf, 1, left)
    for step in range(2, 5):
        k = 5 - step
        moments(k)
        with_sibling(k)
        add_sibling(k)
        order = (0, 1) if step > 2 else (1, 0)
        for c in order:
            pass_on(step, c, 1, rbuf, 0, right)
            pass_on(step, 1 - c if step == 2 else c, -1, lbuf, 1, left)
    moments(0)
    with_sibling(0)
    add_sibling(0)

    def collected(c):
        value = mbuf[m_rows(0, c), :]
        for toward, buf in ((1, rbuf), (-1, lbuf)):
            landed = buf.at[slot(4, c)]
            reduce_copy(base_of[toward] + slot(4, c), landed, landed, right).wait_recv()
            value += landed[...]
        return value

    mbuf[m_rows(0, 1), :] = collected(1)
    push(19, mbuf.at[m_rows(0, 1)], xbuf, partner)
    sums = collected(0)
    reduce_copy(19, xbuf, xbuf, partner).wait_recv()
    sums += xbuf[...]

    counts = jnp.sum(sums[:, 2 * width :], axis=1, keepdims=True)
    kept = 0.4 * mass
    new_mass = kept + 0.6 * mass_scale * counts
    means, variances = mean_ref[...], var_ref[...]
    first = kept * means + 0.6 * mass_scale * sums[:, width : 2 * width]
    second = kept * (variances + means * means) + 0.6 * mass_scale * sums[:, 0:width]
    new_means = first / new_mass
    new_mean_ref[...] = new_means
    new_var_ref[...] = second / new_mass - new_means * new_means
    new_mass_ref[...] = jnp.sum(
        jnp.where(diagonal, jnp.broadcast_to(new_mass, (own, own)), 0.0), axis=0, keepdims=True
    )

    for copy in sent:
        copy.wait_send()

    def stat_sent(t, carry):
        stat_copy(t).wait_send()
        return carry

    lax.fori_loop(1, n_comp, stat_sent, 0)


def solution(mesh):
    n_dp, n_comp = mesh.shape["dp"], mesh.shape["comp"]
    n_z = n_dp // 4

    def per_device(embeddings, comp_means, comp_variances, comp_mass):
        rows, width = embeddings.shape
        own = comp_means.shape[0]
        group = own * n_dp
        wide = 2 * width + 128
        tiles = rows // 128
        f32, bf16 = jnp.float32, jnp.bfloat16
        vmem, dma = pltpu.VMEM, pltpu.SemaphoreType.DMA
        inside = pl.BlockSpec(memory_space=pltpu.VMEM)
        new_means, new_variances, new_mass = pl.pallas_call(
            functools.partial(kernel, n_z, n_comp, (group * n_comp) / (rows * n_dp)),
            out_shape=[
                jax.ShapeDtypeStruct((own, width), f32),
                jax.ShapeDtypeStruct((own, width), f32),
                jax.ShapeDtypeStruct((1, own), f32),
            ],
            in_specs=[pl.BlockSpec(memory_space=pl.ANY), inside, inside, inside],
            out_specs=[inside, inside, inside],
            scratch_shapes=[
                vmem((rows, width), f32),
                vmem((group, wide), f32),
                vmem((16 * own, 2 * width), bf16),
                vmem((group, 128), f32),
                vmem((rows, 2 * width), bf16),
                vmem((rows, 2 * width), bf16),
                vmem((group, rows), f32),
                vmem((n_comp, 2 * tiles, 128), f32),
                vmem((tiles, 128), f32),
                vmem((2 * group, rows), bf16),
                vmem((group, wide), f32),
                vmem((group // 2, wide), f32),
                vmem((7, own, wide), f32),
                vmem((7, own, wide), f32),
                vmem((own, wide), f32),
                dma, dma((31,)), dma((31,)), dma((n_comp,)), dma((n_comp,)), dma((20,)), dma((20,)),
            ],
            compiler_params=pltpu.CompilerParams(
                collective_id=0, has_side_effects=True, vmem_limit_bytes=56 * 1024 * 1024
            ),
        )(embeddings, comp_means, comp_variances, comp_mass.reshape(1, own))
        return new_means, new_variances, new_mass.reshape(own)

    placed = (P("dp", None), P(("comp", "dp"), None), P(("comp", "dp"), None), P(("comp", "dp")))
    return jax.shard_map(
        per_device,
        mesh=mesh,
        in_specs=placed,
        out_specs=(P(("comp", "dp"), None), P(("comp", "dp"), None), P(("comp", "dp"))),
        check_vma=False,
    )
```

time: 530 us -> 84.1 us (0.16)
  waiting for transfers between devices: 273 us -> 0 us
  blocking collectives: 201 us -> 0 us
  Pallas kernels: 0 us -> 79.1 us
  matrix products: 29.6 us -> 0 us
  between operations: 15.2 us -> 0.64 us
    reduce_scatter x2 -> x0, waiting for transfers between devices: 169 us -> none  [the longest x1 128 us: per_device(): lax.psum_scatter(second_sums, 'dp', scatter_dimension=0, tiled=True)]
    unnamed x2 -> x0, blocking collectives: 151 us -> none
    all_gather x2 -> x0, waiting for transfers between devices: 103 us -> none  [the longest x1 84.3 us: per_device(): lax.all_gather(comp_means, 'dp', axis=0, tiled=True)]
    pallas_call x0 -> x1, Pallas kernels: none -> 79.1 us  [per_device(): pl.pallas_call(functools.partial(kernel, n_z, n_comp, group * n_comp / (r...]
    dot_general x4 -> x0, matrix products: 29.6 us -> none  [the longest x2 16.9 us: moments_of(): lax.dot_general(responsibility, values, (((0,), (0,)), ((), ())), precisi...]
    pmax x1 -> x0, blocking collectives: 26.4 us -> none  [per_device(): row_peak = lax.pmax(local_peak, 'comp')]
    psum x1 -> x0, blocking collectives: 23.8 us -> none  [per_device(): row_total = lax.psum(jnp.sum(shifted, axis=1), 'comp')]
  transfers between devices with their start and end apart: 4 -> 0, of which waited for: 4 -> 0; matrix products, arithmetic and copies ran while one was open for 2% -> 0% of each run, Pallas kernels for 0% -> 0%
where the time goes in v1:
time: 84.1 us; the launch traced here: 83.7 us
  Pallas kernels  79.1 us (94%)
  local copies, waits for them, and re-layouts  4.03 us (5%)
    pallas_call x1, Pallas kernels, per_device(): pl.pallas_call(functools.partial(kernel, n_z, n_comp, group * n_comp / (r...  79.1 us
    unnamed x3, local copies, waits for them, and re-layouts  4.03 us

profile of v1, /device:TPU:1, one launch (start us, length us, event | category | flops | bytes accessed | tf_op | source)
XLA Modules:
  0.0 83.7 jit_solution(16191722195416417247)
XLA Ops:
  0.6 79.1 %shard_map.67 = (f32[16,768]{1,0:T(8,128)}, f32[16,768]{1,0:T(8,128)}, f32[1,16]{1,0:T(1,128)}) custom-call(f32[1024,768]{1,0:T(8,128)} %emb_hbm.1, f32[16,768]{1,0:T(8,128)} %mean_ref.1, f32[16,768]{1,0:T(8,128)} %var_ref.1, f32[1,16]{1,0:T(1,128)} %bitcast.2), custom_call_target="tpu_custom_call" | custom-call | tf_op jit(solution)/shard_map/pallas_call | solution.py:376
  79.7 1.4 %copy.10 = f32[16,768]{1,0:T(8,128)} copy(f32[16,768]{1,0:T(8,128)} %get-tuple-element.12) | data formatting | bytes 98304
  81.1 1.4 %copy.11 = f32[16,768]{1,0:T(8,128)} copy(f32[16,768]{1,0:T(8,128)} %get-tuple-element.13) | data formatting | bytes 98304
  82.6 1.2 %copy.12 = f32[16]{0:T(128)} copy(f32[16]{0:T(128)} %bitcast.3) | data formatting | bytes 128

commit v2 on v1

v2 whole, which is shorter than its diff:
```python
import functools

import jax
import jax.numpy as jnp
from jax import lax
from jax.experimental import pallas as pl
from jax.experimental.pallas import tpu as pltpu
from jax.sharding import PartitionSpec as P

MESH = pl.DeviceIdType.MESH
NT = (((1,), (1,)), ((), ()))
NN = (((1,), (0,)), ((), ()))


def split(value):
    high = value.astype(jnp.bfloat16)
    return high, (value - high.astype(jnp.float32)).astype(jnp.bfloat16)


def diagonal(n):
    return lax.broadcasted_iota(jnp.int32, (n, n), 0) == lax.broadcasted_iota(jnp.int32, (n, n), 1)


def column(row):
    n = row.shape[1]
    return jnp.sum(jnp.where(diagonal(n), jnp.broadcast_to(row, (n, n)), 0.0), axis=1, keepdims=True)


def update(
    mass_scale, sums_ref, mean_ref, var_ref, mass_ref, new_mean_ref, new_var_ref, new_mass_ref
):
    own, width = mean_ref.shape
    mass = column(mass_ref[...])
    counts = jnp.sum(sums_ref[:, 2 * width :], axis=1, keepdims=True)
    kept = 0.4 * mass
    new_mass = kept + 0.6 * mass_scale * counts
    means, variances = mean_ref[...], var_ref[...]
    first = kept * means + 0.6 * mass_scale * sums_ref[:, width : 2 * width]
    second = kept * (variances + means * means) + 0.6 * mass_scale * sums_ref[:, 0:width]
    new_means = first / new_mass
    new_mean_ref[...] = new_means
    new_var_ref[...] = second / new_mass - new_means * new_means
    new_mass_ref[...] = jnp.sum(
        jnp.where(diagonal(own), jnp.broadcast_to(new_mass, (own, own)), 0.0), axis=0, keepdims=True
    )


def kernel(
    n_z, n_comp,
    emb_hbm, mean_ref, var_ref, mass_ref,
    sums_ref,
    emb, wbuf, lhs, offs, xx_hi, xx_lo, st, stats, fac, rt,
    mbuf, sbuf, zbuf, xbuf,
    emb_sem, gs, gr, ss, sr, ms, mr,
):
    f32 = jnp.float32
    rows, width = emb.shape
    own = mean_ref.shape[0]
    part = own // 2
    chunk = 2 * own
    half = n_z * chunk
    tiles = rows // 128
    dp, comp = lax.axis_index("dp"), lax.axis_index("comp")
    z, xh, core = dp // 4, (dp // 2) % 2, dp % 2
    other_x, other_core = 1 - xh, 1 - core

    def at(zz, xx, cc):
        return (zz * 4 + xx * 2 + cc, comp)

    def z_off(k):
        return (z + k + n_z) % n_z

    right, left = at(z_off(1), xh, core), at(z_off(-1), xh, core)
    right2, left2 = at(z_off(2), xh, core), at(z_off(-2), xh, core)
    partner = (z * 4 + other_x * 2 + core, (comp + n_comp // 2) % n_comp)
    sibling = at(z, xh, other_core)

    emb_copy = pltpu.make_async_copy(emb_hbm, emb, emb_sem)
    emb_copy.start()
    barrier = pltpu.get_barrier_semaphore()
    for target in (right, left, right2, left2, partner, sibling):
        pl.semaphore_signal(barrier, inc=1, device_id=target, device_id_type=MESH)

    def greet(t, carry):
        peer = (dp, (comp + t) % n_comp)
        pl.semaphore_signal(barrier, inc=1, device_id=peer, device_id_type=MESH)
        return carry

    lax.fori_loop(1, n_comp, greet, 0)

    means, variances = mean_ref[...], var_ref[...]
    precision = 1.0 / variances
    mean_prec = means * precision
    mass = column(mass_ref[...])
    offset = jnp.log(mass) - 0.5 * jnp.sum(
        jnp.log(variances) + means * mean_prec, axis=1, keepdims=True
    )

    def w_rows(cc, zz, xx):
        return pl.ds(pl.multiple_of(cc * half + zz * chunk + xx * own, own), own)

    mine = w_rows(core, z, xh)
    wbuf[mine, 0:width] = -0.5 * precision
    wbuf[mine, width : 2 * width] = mean_prec
    wbuf[mine, 2 * width :] = jnp.broadcast_to(offset, (own, 128))

    pl.semaphore_wait(barrier, 6 + n_comp - 1)

    cols = (xh, other_x)
    sent = []

    def gather_copy(index, k, c, p, target, n=part):
        start = core * half + z_off(k) * chunk + (cols[c] * own if n < chunk else 0) + p * part
        place = pl.ds(pl.multiple_of(start, part), n)
        return pltpu.make_async_remote_copy(
            src_ref=wbuf.at[place], dst_ref=wbuf.at[place],
            send_sem=gs.at[index], recv_sem=gr.at[index],
            device_id=target, device_id_type=MESH,
        )

    def send(index, k, c, p, target, n=part):
        copy = gather_copy(index, k, c, p, target, n)
        copy.start()
        sent.append(copy)

    def arrived(index, n=part):
        gather_copy(index, 0, 0, 0, partner, n).wait_recv()

    A, B, Q = 0, 1, 2
    item = {A: (0, 0), B: (0, 1), Q: (1, 0)}

    def ring(toward, step, it):
        return (0 if toward > 0 else 10) + ((step - 1) * 3 + it if step < 4 else 9)

    def around(toward, step, it):
        far = step == 4
        target = ((right2 if far else right) if toward > 0 else (left2 if far else left))
        send(ring(toward, step, it), -toward * (2 if far else step - 1), *item[it], target)

    def came(toward, step, it):
        arrived(ring(toward, step, it))

    def x_index(k, p):
        return 20 + {(0, 0): 0, (0, 1): 1, (4, 0): 8, (4, 1): 9}.get((k, p), 1 + 2 * abs(k) - (k < 0))

    def across(k, p):
        send(x_index(k, p), k, 0, p, partner)

    def crossed(k, p):
        arrived(x_index(k, p))

    def to_sibling(k):
        send(30 + k % 8, k, 0, 0, sibling, chunk)

    around(1, 1, A)
    around(-1, 1, B)
    across(0, 0)

    emb_copy.wait()

    def prepare(i, carry):
        place = pl.ds(pl.multiple_of(i * 128, 128), 128)
        x = emb[place, :]
        hi, lo = split(x * x)
        xx_hi[place, 0:width] = hi
        xx_lo[place, 0:width] = lo
        hi, lo = split(x)
        xx_hi[place, width:] = hi
        xx_lo[place, width:] = lo
        return carry

    lax.fori_loop(0, tiles // 2, prepare, 0)
    around(1, 1, B)
    around(-1, 1, A)
    across(0, 1)
    lax.fori_loop(tiles // 2, tiles, prepare, 0)

    groups = ((0, -1, 1), (-2, 2), (-3, 3, 4))
    bases = [2 * chunk * sum(len(g) for g in groups[:i]) for i in range(3)]

    def stage(g):
        n, base = 2 * chunk * len(groups[g]), bases[g]
        places = [(cc, z_off(k)) for cc in (core, other_core) for k in groups[g]]
        for i, (cc, zz) in enumerate(places):
            place = pl.ds(pl.multiple_of(cc * half + zz * chunk, chunk), chunk)
            hi, lo = split(wbuf[place, 0 : 2 * width])
            lhs[i * chunk : (i + 1) * chunk, :] = hi
            lhs[n + i * chunk : n + (i + 1) * chunk, :] = lo
            offs[base + i * chunk : base + (i + 1) * chunk, :] = wbuf[place, 2 * width :]

    block = 256
    blocks = rows // block

    def score(g, first, last):
        n, base = 2 * chunk * len(groups[g]), bases[g]

        def body(b, carry):
            place = pl.ds(pl.multiple_of(b * block, block), block)
            both = lax.dot_general(
                lhs[0 : 2 * n, :], xx_hi[place, :], NT, preferred_element_type=f32
            )
            low = lax.dot_general(lhs[0:n, :], xx_lo[place, :], NT, preferred_element_type=f32)
            off = offs[base : base + n, :]
            st[base : base + n, place] = both[:n] + both[n:] + low + jnp.concatenate([off, off], 1)
            return carry

        lax.fori_loop(first, last, body, 0)

    def sibling_arrived(g):
        for k in groups[g]:
            arrived(30 + k % 8, chunk)

    came(1, 1, A)
    around(1, 2, A)
    came(-1, 1, B)
    around(-1, 2, B)
    across(1, 1)
    crossed(0, 0)
    around(1, 1, Q)
    around(-1, 1, Q)
    came(1, 1, B)
    around(1, 2, B)
    across(-1, 1)
    came(-1, 1, A)
    around(-1, 2, A)
    crossed(0, 1)
    to_sibling(0)
    came(1, 2, A)
    around(1, 4, A)
    around(1, 3, A)
    came(-1, 2, B)
    around(-1, 4, B)
    around(-1, 3, B)
    across(2, 1)
    came(1, 1, Q)
    around(1, 2, Q)
    came(-1, 1, Q)
    around(-1, 2, Q)
    crossed(1, 1)
    to_sibling(1)
    came(1, 2, B)
    around(1, 3, B)
    across(-2, 1)
    came(-1, 2, A)
    around(-1, 3, A)
    crossed(-1, 1)
    to_sibling(-1)
    sibling_arrived(0)
    stage(0)
    score(0, 0, blocks // 2)
    came(1, 2, Q)
    around(1, 3, Q)
    came(-1, 2, Q)
    around(-1, 3, Q)
    came(-1, 3, B)
    across(3, 1)
    crossed(2, 1)
    to_sibling(2)
    came(1, 4, A)
    across(4, 0)
    came(-1, 4, B)
    across(4, 1)
    came(1, 3, B)
    across(-3, 1)
    crossed(-2, 1)
    to_sibling(-2)
    score(0, blocks // 2, blocks)
    sibling_arrived(1)
    stage(1)
    score(1, 0, blocks // 2)
    came(1, 3, A)
    came(-1, 3, A)
    came(1, 3, Q)
    came(-1, 3, Q)
    crossed(3, 1)
    to_sibling(3)
    crossed(-3, 1)
    to_sibling(-3)
    score(1, blocks // 2, blocks)
    crossed(4, 0)
    crossed(4, 1)
    to_sibling(4)
    sibling_arrived(2)
    stage(2)
    score(2, 0, blocks)

    for i in range(tiles):
        lanes = slice(i * 128, (i + 1) * 128)
        s = st[:, lanes]
        peak = jnp.max(s, axis=0, keepdims=True)
        e = jnp.exp(s - peak)
        st[:, lanes] = e
        stats[comp, i : i + 1, :] = peak
        stats[comp, tiles + i : tiles + i + 1, :] = jnp.sum(e, axis=0, keepdims=True)

    def stat_copy(t):
        return pltpu.make_async_remote_copy(
            src_ref=stats.at[comp], dst_ref=stats.at[comp],
            send_sem=ss.at[t], recv_sem=sr.at[t],
            device_id=(dp, (comp + t) % n_comp), device_id_type=MESH,
        )

    def stat_start(t, carry):
        stat_copy(t).start()
        return carry

    def stat_wait(t, carry):
        stat_copy(t).wait_recv()
        return carry

    lax.fori_loop(1, n_comp, stat_start, 0)
    lax.fori_loop(1, n_comp, stat_wait, 0)
    peaks, totals = stats[:, 0:tiles, :], stats[:, tiles:, :]
    peak = jnp.max(peaks, axis=0)
    total = jnp.sum(totals * jnp.exp(peaks - peak[None]), axis=0)
    fac[...] = jnp.exp(stats[comp, 0:tiles, :] - peak) / total

    counts = None
    for i in range(tiles):
        lanes = slice(i * 128, (i + 1) * 128)
        resp = st[:, lanes] * fac[i : i + 1, :]
        counts = resp if counts is None else counts + resp
        hi, lo = split(resp)
        for g, base in zip(groups, bases):
            n = 2 * chunk * len(g)
            rt[2 * base : 2 * base + n, lanes] = hi[base : base + n]
            rt[2 * base + n : 2 * base + 2 * n, lanes] = lo[base : base + n]
    mbuf[:, 2 * width :] = counts

    def moments(g, first, last):
        n, base = 2 * chunk * len(groups[g]), bases[g]

        def body(b, carry):
            lanes = pl.ds(pl.multiple_of(b * block, block), block)
            both = lax.dot_general(
                rt[2 * base : 2 * base + 2 * n, :], xx_hi[:, lanes], NN, preferred_element_type=f32
            )
            low = lax.dot_general(
                rt[2 * base : 2 * base + n, :], xx_lo[:, lanes], NN, preferred_element_type=f32
            )
            mbuf[base : base + n, lanes] = both[:n] + both[n:] + low
            return carry

        lax.fori_loop(first, last, body, 0)

    def reduce_copy(index, src, dst, target):
        return pltpu.make_async_remote_copy(
            src_ref=src, dst_ref=dst, send_sem=ms.at[index], recv_sem=mr.at[index],
            device_id=target, device_id_type=MESH,
        )

    def push(index, src, dst, target):
        copy = reduce_copy(index, src, dst, target)
        copy.start()
        sent.append(copy)

    def landed(index, dst):
        reduce_copy(index, dst, dst, partner).wait_recv()

    lanes_of = (slice(0, width), slice(width, 2 * width + 128))

    def spot(g, i):
        h, base = chunk * len(groups[g]), bases[g]
        return sbuf.at[base // 2 : base // 2 + h, lanes_of[i]]

    def moments_half(g, i):
        h, base, steps = chunk * len(groups[g]), bases[g], 2 * width // block
        moments(g, i * steps // 2, (i + 1) * steps // 2)
        push(30 + 2 * g + i, mbuf.at[base + h : base + 2 * h, lanes_of[i]], spot(g, i), sibling)

    def add_sibling(g):
        h, base = chunk * len(groups[g]), bases[g]
        for i in range(2):
            landed(30 + 2 * g + i, spot(g, i))
            mbuf[base : base + h, lanes_of[i]] += spot(g, i)[...]

    def m_rows(k, c, p):
        g = [i for i in range(3) if k in groups[i]][0]
        start = bases[g] + groups[g].index(k) * chunk + cols[c] * own + p * part
        return pl.ds(pl.multiple_of(start, part), part)

    def give(k, p):
        i = x_index(k, p)
        push(i, mbuf.at[m_rows(k, 1, p)], xbuf.at[i - 20], partner)

    def take(k, p):
        i = x_index(k, p)
        landed(i, xbuf.at[i - 20])
        mbuf[m_rows(k, 0, p), :] += xbuf[i - 20]

    def r_index(toward, step, it):
        return (0 if toward > 0 else 10) + ((step - 2) * 3 + it if step > 1 else 9)

    def begin(toward, step, it):
        i = r_index(toward, step, it)
        if step == 1:
            src, target = mbuf.at[m_rows(4, *item[it])], right2 if toward > 0 else left2
        else:
            src, target = mbuf.at[m_rows(toward * 3, *item[it])], right if toward > 0 else left
        push(i, src, zbuf.at[i], target)

    def extend(toward, step, it):
        i, j = r_index(toward, step - 1, it), r_index(toward, step, it)
        landed(i, zbuf.at[i])
        value = zbuf[i] + mbuf[m_rows(toward * (5 - step), *item[it]), :]
        if step == 3 and it == (A if toward > 0 else B):
            far = r_index(toward, 1, it)
            landed(far, zbuf.at[far])
            value += zbuf[far]
        zbuf[i] = value
        push(j, zbuf.at[i], zbuf.at[j], right if toward > 0 else left)

    def finish(it):
        place = m_rows(0, *item[it])
        value = mbuf[place, :]
        for toward in (1, -1):
            i = r_index(toward, 4, it)
            landed(i, zbuf.at[i])
            value += zbuf[i]
        return value

    moments_half(2, 0)
    moments_half(2, 1)
    moments_half(1, 0)
    add_sibling(2)
    give(4, 0)
    give(4, 1)
    give(3, 1)
    give(-3, 1)
    begin(1, 2, Q)
    begin(-1, 2, Q)
    begin(1, 2, A)
    begin(-1, 2, A)
    moments_half(1, 1)
    add_sibling(1)
    give(2, 1)
    give(-2, 1)
    take(4, 0)
    begin(1, 1, A)
    take(4, 1)
    begin(-1, 1, B)
    take(3, 1)
    begin(1, 2, B)
    take(-3, 1)
    begin(-1, 2, B)
    moments_half(0, 0)
    extend(1, 3, Q)
    extend(-1, 3, Q)
    extend(-1, 3, A)
    take(2, 1)
    take(-2, 1)
    moments_half(0, 1)
    extend(1, 3, B)
    extend(1, 3, A)
    extend(-1, 3, B)
    add_sibling(0)
    give(1, 1)
    give(-1, 1)
    give(0, 1)
    extend(1, 4, Q)
    extend(-1, 4, Q)
    extend(-1, 4, A)
    take(1, 1)
    extend(1, 4, B)
    extend(1, 4, A)
    take(-1, 1)
    extend(-1, 4, B)
    take(0, 1)
    mbuf[m_rows(0, 1, 0), :] = finish(Q)
    give(0, 0)
    sums_ref[part:, :] = finish(B)
    last = finish(A)
    landed(20, xbuf.at[0])
    sums_ref[0:part, :] = last + xbuf[0]

    for copy in sent:
        copy.wait_send()

    def stat_sent(t, carry):
        stat_copy(t).wait_send()
        return carry

    lax.fori_loop(1, n_comp, stat_sent, 0)


def solution(mesh):
    n_dp, n_comp = mesh.shape["dp"], mesh.shape["comp"]
    n_z = n_dp // 4

    def per_device(embeddings, comp_means, comp_variances, comp_mass):
        rows, width = embeddings.shape
        own = comp_means.shape[0]
        group = own * n_dp
        wide = 2 * width + 128
        tiles = rows // 128
        f32, bf16 = jnp.float32, jnp.bfloat16
        vmem, dma = pltpu.VMEM, pltpu.SemaphoreType.DMA
        inside = pl.BlockSpec(memory_space=pltpu.VMEM)
        mass = comp_mass.reshape(1, own)
        sums = pl.pallas_call(
            functools.partial(kernel, n_z, n_comp),
            out_shape=jax.ShapeDtypeStruct((own, wide), f32),
            in_specs=[pl.BlockSpec(memory_space=pl.ANY), inside, inside, inside],
            out_specs=inside,
            scratch_shapes=[
                vmem((rows, width), f32),
                vmem((group, wide), f32),
                vmem((24 * own, 2 * width), bf16),
                vmem((group, 128), f32),
                vmem((rows, 2 * width), bf16),
                vmem((rows, 2 * width), bf16),
                vmem((group, rows), f32),
                vmem((n_comp, 2 * tiles, 128), f32),
                vmem((tiles, 128), f32),
                vmem((2 * group, rows), bf16),
                vmem((group, wide), f32),
                vmem((group // 2, wide), f32),
                vmem((20, own // 2, wide), f32),
                vmem((10, own // 2, wide), f32),
                dma, dma((38,)), dma((38,)), dma((n_comp,)), dma((n_comp,)), dma((36,)), dma((36,)),
            ],
            compiler_params=pltpu.CompilerParams(
                collective_id=0, has_side_effects=True, vmem_limit_bytes=56 * 1024 * 1024
            ),
        )(embeddings, comp_means, comp_variances, mass)
        new_means, new_variances, new_mass = pl.pallas_call(
            functools.partial(update, (group * n_comp) / (rows * n_dp)),
            out_shape=[
                jax.ShapeDtypeStruct((own, width), f32),
                jax.ShapeDtypeStruct((own, width), f32),
                jax.ShapeDtypeStruct((1, own), f32),
            ],
            in_specs=[inside] * 4,
            out_specs=[inside] * 3,
        )(sums, comp_means, comp_variances, mass)
        return new_means, new_variances, new_mass.reshape(own)

    placed = (P("dp", None), P(("comp", "dp"), None), P(("comp", "dp"), None), P(("comp", "dp")))
    return jax.shard_map(
        per_device,
        mesh=mesh,
        in_specs=placed,
        out_specs=(P(("comp", "dp"), None), P(("comp", "dp"), None), P(("comp", "dp"))),
        check_vma=False,
    )
```

time: 84.1 us -> 79.5 us (0.945)
  local copies, waits for them, and re-layouts: 4.03 us -> 0 us
    unnamed x3 -> x0, local copies, waits for them, and re-layouts: 4.03 us -> none
    pallas_call x1 -> x2, Pallas kernels: 79.1 us -> 78.6 us  [the longest x1 77 us: per_device(): pl.pallas_call(functools.partial(kernel, n_z, n_comp), out_shape=jax.Shap...]
where the time goes in v2:
time: 79.5 us; the launch traced here: 79.3 us
  Pallas kernels  78.6 us (99%)
    pallas_call x1, Pallas kernels, per_device(): pl.pallas_call(functools.partial(kernel, n_z, n_comp), out_shape=jax.Shap...  77 us
    pallas_call x1, Pallas kernels, per_device(): pl.pallas_call(functools.partial(update, group * n_comp / (rows * n_dp)),...  1.66 us

profile of v2, /device:TPU:1, one launch (start us, length us, event | category | flops | bytes accessed | tf_op | source)
XLA Modules:
  0.0 79.3 jit_solution(16826151297252478861)
XLA Ops:
  0.6 77.0 %shard_map.67.sums_ref = f32[16,1664]{1,0:T(8,128)} custom-call(f32[1024,768]{1,0:T(8,128)} %emb_hbm.1, f32[16,768]{1,0:T(8,128)} %mean_ref.3, f32[16,768]{1,0:T(8,128)} %var_ref.3, f32[1,16]{1,0:T(1,128)} %bitcast.2), custom_call_target="tpu_custom_call" | custom-call | tf_op jit(solution)/shard_map/pallas_call | solution.py:500
  77.6 1.7 %shard_map.68 = (f32[16,768]{1,0:T(8,128)}, f32[16,768]{1,0:T(8,128)}, f32[1,16]{1,0:T(1,128)}) custom-call(f32[16,1664]{1,0:T(8,128)} %shard_map.67.sums_ref, f32[16,768]{1,0:T(8,128)} %mean_ref.3, f32[16,768]{1,0:T(8,128)} %var_ref.3, f32[1,16]{1,0:T(1,128)} %bitcast.3), custom_call_target="tpu_custom_call" | custom-call | tf_op jit(solution)/shard_map/pallas_call | solution.py:526

commit v3 on v2

--- a/solution.py
+++ b/solution.py
@@ -126,10 +126,12 @@
     def arrived(index, n=part):
         gather_copy(index, 0, 0, 0, partner, n).wait_recv()
 
-    A, B, Q = 0, 1, 2
-    item = {A: (0, 0), B: (0, 1), Q: (1, 0)}
+    A, B, Q, S = 0, 1, 2, 3
+    item = {A: (0, 0), B: (0, 1), Q: (1, 0), S: (1, 1)}
 
     def ring(toward, step, it):
+        if it == S:
+            return 38 if toward > 0 else 39
         return (0 if toward > 0 else 10) + ((step - 1) * 3 + it if step < 4 else 9)
 
     def around(toward, step, it):
@@ -188,23 +190,16 @@
             lhs[n + i * chunk : n + (i + 1) * chunk, :] = lo
             offs[base + i * chunk : base + (i + 1) * chunk, :] = wbuf[place, 2 * width :]
 
-    block = 256
-    blocks = rows // block
-
-    def score(g, first, last):
+    def score(g, first, last, block):
         n, base = 2 * chunk * len(groups[g]), bases[g]
-
-        def body(b, carry):
-            place = pl.ds(pl.multiple_of(b * block, block), block)
+        for b in range(first, last, block):
+            place = slice(b, b + block)
             both = lax.dot_general(
                 lhs[0 : 2 * n, :], xx_hi[place, :], NT, preferred_element_type=f32
             )
             low = lax.dot_general(lhs[0:n, :], xx_lo[place, :], NT, preferred_element_type=f32)
-            off = offs[base : base + n, :]
-            st[base : base + n, place] = both[:n] + both[n:] + low + jnp.concatenate([off, off], 1)
-            return carry
-
-        lax.fori_loop(first, last, body, 0)
+            off = jnp.concatenate([offs[base : base + n, :]] * (block // 128), 1)
+            st[base : base + n, place] = both[:n] + both[n:] + low + off
 
     def sibling_arrived(g):
         for k in groups[g]:
@@ -227,10 +222,8 @@
     to_sibling(0)
     came(1, 2, A)
     around(1, 4, A)
-    around(1, 3, A)
     came(-1, 2, B)
     around(-1, 4, B)
-    around(-1, 3, B)
     across(2, 1)
     came(1, 1, Q)
     around(1, 2, Q)
@@ -239,50 +232,52 @@
     crossed(1, 1)
     to_sibling(1)
     came(1, 2, B)
-    around(1, 3, B)
     across(-2, 1)
     came(-1, 2, A)
+    around(1, 3, A)
+    around(-1, 3, B)
+    around(1, 3, B)
     around(-1, 3, A)
     crossed(-1, 1)
     to_sibling(-1)
     sibling_arrived(0)
     stage(0)
-    score(0, 0, blocks // 2)
+    score(0, 0, rows // 2, rows // 2)
     came(1, 2, Q)
     around(1, 3, Q)
     came(-1, 2, Q)
     around(-1, 3, Q)
     came(-1, 3, B)
-    across(3, 1)
     crossed(2, 1)
+    around(-1, 3, S)
     to_sibling(2)
     came(1, 4, A)
     across(4, 0)
     came(-1, 4, B)
     across(4, 1)
     came(1, 3, B)
-    across(-3, 1)
     crossed(-2, 1)
+    around(1, 3, S)
     to_sibling(-2)
-    score(0, blocks // 2, blocks)
+    score(0, rows // 2, rows, rows // 2)
     sibling_arrived(1)
     stage(1)
-    score(1, 0, blocks // 2)
+    score(1, 0, rows // 2, rows // 2)
     came(1, 3, A)
     came(-1, 3, A)
     came(1, 3, Q)
     came(-1, 3, Q)
-    crossed(3, 1)
+    came(-1, 3, S)
     to_sibling(3)
-    crossed(-3, 1)
+    came(1, 3, S)
     to_sibling(-3)
-    score(1, blocks // 2, blocks)
+    score(1, rows // 2, rows, rows // 2)
     crossed(4, 0)
     crossed(4, 1)
     to_sibling(4)
     sibling_arrived(2)
     stage(2)
-    score(2, 0, blocks)
+    score(2, 0, rows, rows)
 
     for i in range(tiles):
         lanes = slice(i * 128, (i + 1) * 128)
@@ -290,8 +285,8 @@
         peak = jnp.max(s, axis=0, keepdims=True)
         e = jnp.exp(s - peak)
         st[:, lanes] = e
-        stats[comp, i : i + 1, :] = peak
-        stats[comp, tiles + i : tiles + i + 1, :] = jnp.sum(e, axis=0, keepdims=True)
+        fac[i : i + 1, :] = peak
+        stats[comp, i : i + 1, :] = peak + jnp.log(jnp.sum(e, axis=0, keepdims=True))
 
     def stat_copy(t):
         return pltpu.make_async_remote_copy(
@@ -310,10 +305,10 @@
 
     lax.fori_loop(1, n_comp, stat_start, 0)
     lax.fori_loop(1, n_comp, stat_wait, 0)
-    peaks, totals = stats[:, 0:tiles, :], stats[:, tiles:, :]
-    peak = jnp.max(peaks, axis=0)
-    total = jnp.sum(totals * jnp.exp(peaks - peak[None]), axis=0)
-    fac[...] = jnp.exp(stats[comp, 0:tiles, :] - peak) / total
+    logs = stats[...]
+    peak = jnp.max(logs, axis=0)
+    total = jnp.sum(jnp.exp(logs - peak[None]), axis=0)
+    fac[...] = jnp.exp(fac[...] - peak) / total
 
     counts = None
     for i in range(tiles):
@@ -327,21 +322,15 @@
             rt[2 * base + n : 2 * base + 2 * n, lanes] = lo[base : base + n]
     mbuf[:, 2 * width :] = counts
 
-    def moments(g, first, last):
+    def moments(g, lanes):
         n, base = 2 * chunk * len(groups[g]), bases[g]
-
-        def body(b, carry):
-            lanes = pl.ds(pl.multiple_of(b * block, block), block)
-            both = lax.dot_general(
-                rt[2 * base : 2 * base + 2 * n, :], xx_hi[:, lanes], NN, preferred_element_type=f32
-            )
-            low = lax.dot_general(
-                rt[2 * base : 2 * base + n, :], xx_lo[:, lanes], NN, preferred_element_type=f32
-            )
-            mbuf[base : base + n, lanes] = both[:n] + both[n:] + low
-            return carry
-
-        lax.fori_loop(first, last, body, 0)
+        both = lax.dot_general(
+            rt[2 * base : 2 * base + 2 * n, :], xx_hi[:, lanes], NN, preferred_element_type=f32
+        )
+        low = lax.dot_general(
+            rt[2 * base : 2 * base + n, :], xx_lo[:, lanes], NN, preferred_element_type=f32
+        )
+        mbuf[base : base + n, lanes] = both[:n] + both[n:] + low
 
     def reduce_copy(index, src, dst, target):
         return pltpu.make_async_remote_copy(
@@ -364,8 +353,8 @@
         return sbuf.at[base // 2 : base // 2 + h, lanes_of[i]]
 
     def moments_half(g, i):
-        h, base, steps = chunk * len(groups[g]), bases[g], 2 * width // block
-        moments(g, i * steps // 2, (i + 1) * steps // 2)
+        h, base = chunk * len(groups[g]), bases[g]
+        moments(g, slice(i * width, (i + 1) * width))
         push(30 + 2 * g + i, mbuf.at[base + h : base + 2 * h, lanes_of[i]], spot(g, i), sibling)
 
     def add_sibling(g):
@@ -389,6 +378,8 @@
         mbuf[m_rows(k, 0, p), :] += xbuf[i - 20]
 
     def r_index(toward, step, it):
+        if it == S:
+            return 38 if toward > 0 else 39
         return (0 if toward > 0 else 10) + ((step - 2) * 3 + it if step > 1 else 9)
 
     def begin(toward, step, it):
@@ -397,7 +388,7 @@
             src, target = mbuf.at[m_rows(4, *item[it])], right2 if toward > 0 else left2
         else:
             src, target = mbuf.at[m_rows(toward * 3, *item[it])], right if toward > 0 else left
-        push(i, src, zbuf.at[i], target)
+        push(i, src, zbuf.at[i if it < S else i - 18], target)
 
     def extend(toward, step, it):
         i, j = r_index(toward, step - 1, it), r_index(toward, step, it)
@@ -410,6 +401,11 @@
         zbuf[i] = value
         push(j, zbuf.at[i], zbuf.at[j], right if toward > 0 else left)
 
+    def merge(toward):
+        i = r_index(toward, 2, S)
+        landed(i, zbuf.at[i - 18])
+        mbuf[m_rows(2 * toward, 1, 1), :] += zbuf[i - 18]
+
     def finish(it):
         place = m_rows(0, *item[it])
         value = mbuf[place, :]
@@ -425,49 +421,49 @@
     add_sibling(2)
     give(4, 0)
     give(4, 1)
-    give(3, 1)
-    give(-3, 1)
+    begin(1, 2, S)
+    begin(-1, 2, S)
     begin(1, 2, Q)
     begin(-1, 2, Q)
+    moments_half(1, 1)
+    begin(1, 2, B)
+    begin(-1, 2, A)
     begin(1, 2, A)
-    begin(-1, 2, A)
-    moments_half(1, 1)
+    begin(-1, 2, B)
+    moments_half(0, 0)
     add_sibling(1)
+    merge(1)
     give(2, 1)
+    merge(-1)
     give(-2, 1)
     take(4, 0)
     begin(1, 1, A)
     take(4, 1)
     begin(-1, 1, B)
-    take(3, 1)
-    begin(1, 2, B)
-    take(-3, 1)
-    begin(-1, 2, B)
-    moments_half(0, 0)
     extend(1, 3, Q)
     extend(-1, 3, Q)
+    moments_half(0, 1)
     extend(-1, 3, A)
-    take(2, 1)
-    take(-2, 1)
-    moments_half(0, 1)
-    extend(1, 3, B)
-    extend(1, 3, A)
-    extend(-1, 3, B)
     add_sibling(0)
     give(1, 1)
     give(-1, 1)
     give(0, 1)
+    take(2, 1)
+    extend(1, 3, B)
     extend(1, 4, Q)
     extend(-1, 4, Q)
+    extend(1, 3, A)
+    take(-2, 1)
+    extend(-1, 3, B)
     extend(-1, 4, A)
     take(1, 1)
     extend(1, 4, B)
+    mbuf[m_rows(0, 1, 0), :] = finish(Q)
+    give(0, 0)
     extend(1, 4, A)
     take(-1, 1)
     extend(-1, 4, B)
     take(0, 1)
-    mbuf[m_rows(0, 1, 0), :] = finish(Q)
-    give(0, 0)
     sums_ref[part:, :] = finish(B)
     last = finish(A)
     landed(20, xbuf.at[0])
@@ -510,14 +506,14 @@
                 vmem((rows, 2 * width), bf16),
                 vmem((rows, 2 * width), bf16),
                 vmem((group, rows), f32),
-                vmem((n_comp, 2 * tiles, 128), f32),
+                vmem((n_comp, tiles, 128), f32),
                 vmem((tiles, 128), f32),
                 vmem((2 * group, rows), bf16),
                 vmem((group, wide), f32),
                 vmem((group // 2, wide), f32),
-                vmem((20, own // 2, wide), f32),
+                vmem((22, own // 2, wide), f32),
                 vmem((10, own // 2, wide), f32),
-                dma, dma((38,)), dma((38,)), dma((n_comp,)), dma((n_comp,)), dma((36,)), dma((36,)),
+                dma, dma((40,)), dma((40,)), dma((n_comp,)), dma((n_comp,)), dma((40,)), dma((40,)),
             ],
             compiler_params=pltpu.CompilerParams(
                 collective_id=0, has_side_effects=True, vmem_limit_bytes=56 * 1024 * 1024

time: 79.5 us -> 70 us (0.88)
  Pallas kernels: 78.6 us -> 68.6 us
    pallas_call x1, Pallas kernels: 77 us -> 66.9 us  [per_device(): pl.pallas_call(functools.partial(kernel, n_z, n_comp), out_shape=jax.Shap...]
where the time goes in v3:
time: 70 us; the launch traced here: 69.2 us
  Pallas kernels  68.6 us (98%)
    pallas_call x1, Pallas kernels, per_device(): pl.pallas_call(functools.partial(kernel, n_z, n_comp), out_shape=jax.Shap...  66.9 us
    pallas_call x1, Pallas kernels, per_device(): pl.pallas_call(functools.partial(update, group * n_comp / (rows * n_dp)),...  1.66 us

profile of v3, /device:TPU:1, one launch (start us, length us, event | category | flops | bytes accessed | tf_op | source)
XLA Modules:
  0.0 69.2 jit_solution(9728979466169788504)
XLA Ops:
  0.6 66.9 %shard_map.67.sums_ref = f32[16,1664]{1,0:T(8,128)} custom-call(f32[1024,768]{1,0:T(8,128)} %emb_hbm.1, f32[16,768]{1,0:T(8,128)} %mean_ref.3, f32[16,768]{1,0:T(8,128)} %var_ref.3, f32[1,16]{1,0:T(1,128)} %bitcast.2), custom_call_target="tpu_custom_call" | custom-call | tf_op jit(solution)/shard_map/pallas_call | solution.py:496
  67.5 1.7 %shard_map.68 = (f32[16,768]{1,0:T(8,128)}, f32[16,768]{1,0:T(8,128)}, f32[1,16]{1,0:T(1,128)}) custom-call(f32[16,1664]{1,0:T(8,128)} %shard_map.67.sums_ref, f32[16,768]{1,0:T(8,128)} %mean_ref.3, f32[16,768]{1,0:T(8,128)} %var_ref.3, f32[1,16]{1,0:T(1,128)} %bitcast.3), custom_call_target="tpu_custom_call" | custom-call | tf_op jit(solution)/shard_map/pallas_call | solution.py:522

commit v4 on v3

--- a/solution.py
+++ b/solution.py
@@ -31,7 +31,15 @@
 ):
     own, width = mean_ref.shape
     mass = column(mass_ref[...])
-    counts = jnp.sum(sums_ref[:, 2 * width :], axis=1, keepdims=True)
+    part = own // 2
+    tile = sums_ref[part:, 2 * width :]
+    low_lanes = lax.broadcasted_iota(jnp.int32, tile.shape, 1) < 64
+    counts = jnp.concatenate(
+        [
+            jnp.sum(jnp.where(low_lanes, tile, 0.0), axis=1, keepdims=True),
+            jnp.sum(jnp.where(low_lanes, 0.0, tile), axis=1, keepdims=True),
+        ]
+    )
     kept = 0.4 * mass
     new_mass = kept + 0.6 * mass_scale * counts
     means, variances = mean_ref[...], var_ref[...]
@@ -102,7 +110,13 @@
     mine = w_rows(core, z, xh)
     wbuf[mine, 0:width] = -0.5 * precision
     wbuf[mine, width : 2 * width] = mean_prec
-    wbuf[mine, 2 * width :] = jnp.broadcast_to(offset, (own, 128))
+    low_lanes = lax.broadcasted_iota(jnp.int32, (part, 128), 1) < 64
+    second = pl.ds(pl.multiple_of(core * half + z * chunk + xh * own + part, part), part)
+    wbuf[second, 2 * width :] = jnp.where(
+        low_lanes,
+        jnp.broadcast_to(offset[0:part], (part, 128)),
+        jnp.broadcast_to(offset[part:own], (part, 128)),
+    )
 
     pl.semaphore_wait(barrier, 6 + n_comp - 1)
 
@@ -112,8 +126,9 @@
     def gather_copy(index, k, c, p, target, n=part):
         start = core * half + z_off(k) * chunk + (cols[c] * own if n < chunk else 0) + p * part
         place = pl.ds(pl.multiple_of(start, part), n)
+        span = slice(0, 2 * width) if n == part and p == 0 else slice(0, 2 * width + 128)
         return pltpu.make_async_remote_copy(
-            src_ref=wbuf.at[place], dst_ref=wbuf.at[place],
+            src_ref=wbuf.at[place, span], dst_ref=wbuf.at[place, span],
             send_sem=gs.at[index], recv_sem=gr.at[index],
             device_id=target, device_id_type=MESH,
         )
@@ -123,8 +138,8 @@
         copy.start()
         sent.append(copy)
 
-    def arrived(index, n=part):
-        gather_copy(index, 0, 0, 0, partner, n).wait_recv()
+    def arrived(index, p, n=part):
+        gather_copy(index, 0, 0, p, partner, n).wait_recv()
 
     A, B, Q, S = 0, 1, 2, 3
     item = {A: (0, 0), B: (0, 1), Q: (1, 0), S: (1, 1)}
@@ -140,7 +155,7 @@
         send(ring(toward, step, it), -toward * (2 if far else step - 1), *item[it], target)
 
     def came(toward, step, it):
-        arrived(ring(toward, step, it))
+        arrived(ring(toward, step, it), item[it][1])
 
     def x_index(k, p):
         return 20 + {(0, 0): 0, (0, 1): 1, (4, 0): 8, (4, 1): 9}.get((k, p), 1 + 2 * abs(k) - (k < 0))
@@ -149,7 +164,7 @@
         send(x_index(k, p), k, 0, p, partner)
 
     def crossed(k, p):
-        arrived(x_index(k, p))
+        arrived(x_index(k, p), p)
 
     def to_sibling(k):
         send(30 + k % 8, k, 0, 0, sibling, chunk)
@@ -188,7 +203,13 @@
             hi, lo = split(wbuf[place, 0 : 2 * width])
             lhs[i * chunk : (i + 1) * chunk, :] = hi
             lhs[n + i * chunk : n + (i + 1) * chunk, :] = lo
-            offs[base + i * chunk : base + (i + 1) * chunk, :] = wbuf[place, 2 * width :]
+            tile = wbuf[place, 2 * width :]
+            for r in range(0, chunk, part):
+                both = tile[r // own * own + part : r // own * own + own]
+                lane = 64 * (r % own // part)
+                offs[base + i * chunk + r : base + i * chunk + r + part, :] = jnp.broadcast_to(
+                    both[:, lane : lane + 1], (part, 128)
+                )
 
     def score(g, first, last, block):
         n, base = 2 * chunk * len(groups[g]), bases[g]
@@ -203,7 +224,7 @@
 
     def sibling_arrived(g):
         for k in groups[g]:
-            arrived(30 + k % 8, chunk)
+            arrived(30 + k % 8, 0, chunk)
 
     came(1, 1, A)
     around(1, 2, A)
@@ -277,60 +298,71 @@
     to_sibling(4)
     sibling_arrived(2)
     stage(2)
-    score(2, 0, rows, rows)
-
-    for i in range(tiles):
-        lanes = slice(i * 128, (i + 1) * 128)
-        s = st[:, lanes]
-        peak = jnp.max(s, axis=0, keepdims=True)
-        e = jnp.exp(s - peak)
-        st[:, lanes] = e
-        fac[i : i + 1, :] = peak
-        stats[comp, i : i + 1, :] = peak + jnp.log(jnp.sum(e, axis=0, keepdims=True))
-
-    def stat_copy(t):
+
+    def statistic(h):
+        for j in range(tiles // 2):
+            i = h * tiles // 2 + j
+            lanes = slice(i * 128, (i + 1) * 128)
+            s = st[:, lanes]
+            peak = jnp.max(s, axis=0, keepdims=True)
+            e = jnp.exp(s - peak)
+            st[:, lanes] = e
+            fac[i : i + 1, :] = peak
+            stats[h, comp, j : j + 1, :] = peak + jnp.log(jnp.sum(e, axis=0, keepdims=True))
+
+    def stat_copy(h, t):
         return pltpu.make_async_remote_copy(
-            src_ref=stats.at[comp], dst_ref=stats.at[comp],
-            send_sem=ss.at[t], recv_sem=sr.at[t],
+            src_ref=stats.at[h, comp], dst_ref=stats.at[h, comp],
+            send_sem=ss.at[h, t], recv_sem=sr.at[h, t],
             device_id=(dp, (comp + t) % n_comp), device_id_type=MESH,
         )
 
-    def stat_start(t, carry):
-        stat_copy(t).start()
-        return carry
-
-    def stat_wait(t, carry):
-        stat_copy(t).wait_recv()
-        return carry
-
-    lax.fori_loop(1, n_comp, stat_start, 0)
-    lax.fori_loop(1, n_comp, stat_wait, 0)
-    logs = stats[...]
-    peak = jnp.max(logs, axis=0)
-    total = jnp.sum(jnp.exp(logs - peak[None]), axis=0)
-    fac[...] = jnp.exp(fac[...] - peak) / total
-
-    counts = None
-    for i in range(tiles):
-        lanes = slice(i * 128, (i + 1) * 128)
-        resp = st[:, lanes] * fac[i : i + 1, :]
-        counts = resp if counts is None else counts + resp
-        hi, lo = split(resp)
-        for g, base in zip(groups, bases):
-            n = 2 * chunk * len(g)
-            rt[2 * base : 2 * base + n, lanes] = hi[base : base + n]
-            rt[2 * base + n : 2 * base + 2 * n, lanes] = lo[base : base + n]
-    mbuf[:, 2 * width :] = counts
-
-    def moments(g, lanes):
+    def stat_start(h):
+        def body(t, carry):
+            stat_copy(h, t).start()
+            return carry
+
+        lax.fori_loop(1, n_comp, body, 0)
+
+    def responsibilities(h, counts):
+        def body(t, carry):
+            stat_copy(h, t).wait_recv()
+            return carry
+
+        lax.fori_loop(1, n_comp, body, 0)
+        logs = stats[h]
+        peak = jnp.max(logs, axis=0)
+        total = jnp.sum(jnp.exp(logs - peak[None]), axis=0)
+        mine = slice(h * tiles // 2, (h + 1) * tiles // 2)
+        fac[mine, :] = jnp.exp(fac[mine, :] - peak) / total
+        for i in range(h * tiles // 2, (h + 1) * tiles // 2):
+            lanes = slice(i * 128, (i + 1) * 128)
+            resp = st[:, lanes] * fac[i : i + 1, :]
+            counts = resp if counts is None else counts + resp
+            hi, lo = split(resp)
+            for g, base in zip(groups, bases):
+                n = 2 * chunk * len(g)
+                rt[2 * base : 2 * base + n, lanes] = hi[base : base + n]
+                rt[2 * base + n : 2 * base + 2 * n, lanes] = lo[base : base + n]
+        return counts
+
+    score(2, 0, rows // 2, rows // 2)
+    statistic(0)
+    stat_start(0)
+    score(2, rows // 2, rows, rows // 2)
+    statistic(1)
+    stat_start(1)
+
+    def moments(g, lanes, over=slice(None), add=False):
         n, base = 2 * chunk * len(groups[g]), bases[g]
         both = lax.dot_general(
-            rt[2 * base : 2 * base + 2 * n, :], xx_hi[:, lanes], NN, preferred_element_type=f32
+            rt[2 * base : 2 * base + 2 * n, over], xx_hi[over, lanes], NN, preferred_element_type=f32
         )
         low = lax.dot_general(
-            rt[2 * base : 2 * base + n, :], xx_lo[:, lanes], NN, preferred_element_type=f32
-        )
-        mbuf[base : base + n, lanes] = both[:n] + both[n:] + low
+            rt[2 * base : 2 * base + n, over], xx_lo[over, lanes], NN, preferred_element_type=f32
+        )
+        value = both[:n] + both[n:] + low
+        mbuf[base : base + n, lanes] = mbuf[base : base + n, lanes] + value if add else value
 
     def reduce_copy(index, src, dst, target):
         return pltpu.make_async_remote_copy(
@@ -354,7 +386,11 @@
 
     def moments_half(g, i):
         h, base = chunk * len(groups[g]), bases[g]
-        moments(g, slice(i * width, (i + 1) * width))
+        lanes = slice(i * width, (i + 1) * width)
+        if g == 2:
+            moments(g, lanes, slice(rows // 2, rows), True)
+        else:
+            moments(g, lanes)
         push(30 + 2 * g + i, mbuf.at[base + h : base + 2 * h, lanes_of[i]], spot(g, i), sibling)
 
     def add_sibling(g):
@@ -363,19 +399,30 @@
             landed(30 + 2 * g + i, spot(g, i))
             mbuf[base : base + h, lanes_of[i]] += spot(g, i)[...]
 
+    def span(p):
+        return slice(0, 2 * width + (128 if p else 0))
+
+    def z_slot(toward, step, it):
+        i = r_index(toward, step, it)
+        return zbuf.at[i if it < S else i - 18, :, span(item[it][1])]
+
     def m_rows(k, c, p):
         g = [i for i in range(3) if k in groups[i]][0]
         start = bases[g] + groups[g].index(k) * chunk + cols[c] * own + p * part
         return pl.ds(pl.multiple_of(start, part), part)
 
+    def m_part(k, c, p):
+        return mbuf.at[m_rows(k, c, p), span(p)]
+
     def give(k, p):
         i = x_index(k, p)
-        push(i, mbuf.at[m_rows(k, 1, p)], xbuf.at[i - 20], partner)
+        push(i, m_part(k, 1, p), xbuf.at[i - 20, :, span(p)], partner)
 
     def take(k, p):
         i = x_index(k, p)
-        landed(i, xbuf.at[i - 20])
-        mbuf[m_rows(k, 0, p), :] += xbuf[i - 20]
+        here = xbuf.at[i - 20, :, span(p)]
+        landed(i, here)
+        m_part(k, 0, p)[...] += here[...]
 
     def r_index(toward, step, it):
         if it == S:
@@ -383,38 +430,47 @@
         return (0 if toward > 0 else 10) + ((step - 2) * 3 + it if step > 1 else 9)
 
     def begin(toward, step, it):
-        i = r_index(toward, step, it)
-        if step == 1:
-            src, target = mbuf.at[m_rows(4, *item[it])], right2 if toward > 0 else left2
-        else:
-            src, target = mbuf.at[m_rows(toward * 3, *item[it])], right if toward > 0 else left
-        push(i, src, zbuf.at[i if it < S else i - 18], target)
+        far = step == 1
+        target = ((right2 if far else right) if toward > 0 else (left2 if far else left))
+        k = 4 if far else toward * (5 - step)
+        push(r_index(toward, step, it), m_part(k, *item[it]), z_slot(toward, step, it), target)
 
     def extend(toward, step, it):
-        i, j = r_index(toward, step - 1, it), r_index(toward, step, it)
-        landed(i, zbuf.at[i])
-        value = zbuf[i] + mbuf[m_rows(toward * (5 - step), *item[it]), :]
+        here = z_slot(toward, step - 1, it)
+        landed(r_index(toward, step - 1, it), here)
+        value = here[...] + m_part(toward * (5 - step), *item[it])[...]
         if step == 3 and it == (A if toward > 0 else B):
-            far = r_index(toward, 1, it)
-            landed(far, zbuf.at[far])
-            value += zbuf[far]
-        zbuf[i] = value
-        push(j, zbuf.at[i], zbuf.at[j], right if toward > 0 else left)
+            far = z_slot(toward, 1, it)
+            landed(r_index(toward, 1, it), far)
+            value += far[...]
+        here[...] = value
+        push(
+            r_index(toward, step, it), here, z_slot(toward, step, it), right if toward > 0 else left
+        )
 
     def merge(toward):
-        i = r_index(toward, 2, S)
-        landed(i, zbuf.at[i - 18])
-        mbuf[m_rows(2 * toward, 1, 1), :] += zbuf[i - 18]
+        here = z_slot(toward, 2, S)
+        landed(r_index(toward, 2, S), here)
+        m_part(2 * toward, 1, 1)[...] += here[...]
 
     def finish(it):
-        place = m_rows(0, *item[it])
-        value = mbuf[place, :]
+        value = m_part(0, *item[it])[...]
         for toward in (1, -1):
-            i = r_index(toward, 4, it)
-            landed(i, zbuf.at[i])
-            value += zbuf[i]
+            here = z_slot(toward, 4, it)
+            landed(r_index(toward, 4, it), here)
+            value += here[...]
         return value
 
+    counts = responsibilities(0, None)
+    for i in range(2):
+        moments(2, slice(i * width, (i + 1) * width), slice(0, rows // 2))
+    counts = responsibilities(1, counts)
+    counts = counts + pltpu.roll(counts, 64, 1)
+    mbuf[:, 2 * width :] = counts
+    for i in range(0, n_z * 2 * chunk, own):
+        mbuf[i + part : i + own, 2 * width :] = jnp.where(
+            low_lanes, counts[i : i + part], counts[i + part : i + own]
+        )
     moments_half(2, 0)
     moments_half(2, 1)
     moments_half(1, 0)
@@ -458,7 +514,7 @@
     extend(-1, 4, A)
     take(1, 1)
     extend(1, 4, B)
-    mbuf[m_rows(0, 1, 0), :] = finish(Q)
+    m_part(0, 1, 0)[...] = finish(Q)
     give(0, 0)
     extend(1, 4, A)
     take(-1, 1)
@@ -466,14 +522,16 @@
     take(0, 1)
     sums_ref[part:, :] = finish(B)
     last = finish(A)
-    landed(20, xbuf.at[0])
-    sums_ref[0:part, :] = last + xbuf[0]
+    here = xbuf.at[0, :, span(0)]
+    landed(20, here)
+    sums_ref[0:part, 0 : 2 * width] = last + here[...]
 
     for copy in sent:
         copy.wait_send()
 
     def stat_sent(t, carry):
-        stat_copy(t).wait_send()
+        stat_copy(0, t).wait_send()
+        stat_copy(1, t).wait_send()
         return carry
 
     lax.fori_loop(1, n_comp, stat_sent, 0)
@@ -506,14 +564,14 @@
                 vmem((rows, 2 * width), bf16),
                 vmem((rows, 2 * width), bf16),
                 vmem((group, rows), f32),
-                vmem((n_comp, tiles, 128), f32),
+                vmem((2, n_comp, tiles // 2, 128), f32),
                 vmem((tiles, 128), f32),
                 vmem((2 * group, rows), bf16),
                 vmem((group, wide), f32),
                 vmem((group // 2, wide), f32),
                 vmem((22, own // 2, wide), f32),
                 vmem((10, own // 2, wide), f32),
-                dma, dma((40,)), dma((40,)), dma((n_comp,)), dma((n_comp,)), dma((40,)), dma((40,)),
+                dma, dma((40,)), dma((40,)), dma((2, n_comp)), dma((2, n_comp)), dma((40,)), dma((40,)),
             ],
             compiler_params=pltpu.CompilerParams(
                 collective_id=0, has_side_effects=True, vmem_limit_bytes=56 * 1024 * 1024

time: 70 us -> 68.3 us (0.976)
  Pallas kernels: 68.6 us -> 67.5 us
    pallas_call x1, Pallas kernels: 66.9 us -> 65.7 us  [per_device(): pl.pallas_call(functools.partial(kernel, n_z, n_comp), out_shape=jax.Shap...]
where the time goes in v4:
time: 68.3 us; the launch traced here: 68.1 us
  Pallas kernels  67.5 us (99%)
    pallas_call x1, Pallas kernels, per_device(): pl.pallas_call(functools.partial(kernel, n_z, n_comp), out_shape=jax.Shap...  65.7 us
    pallas_call x1, Pallas kernels, per_device(): pl.pallas_call(functools.partial(update, group * n_comp / (rows * n_dp)),...  1.74 us

profile of v4, /device:TPU:1, one launch (start us, length us, event | category | flops | bytes accessed | tf_op | source)
XLA Modules:
  0.0 68.1 jit_solution(13600387279751909790)
XLA Ops:
  0.6 65.7 %shard_map.67.sums_ref = f32[16,1664]{1,0:T(8,128)} custom-call(f32[1024,768]{1,0:T(8,128)} %emb_hbm.1, f32[16,768]{1,0:T(8,128)} %mean_ref.3, f32[16,768]{1,0:T(8,128)} %var_ref.3, f32[1,16]{1,0:T(1,128)} %bitcast.2), custom_call_target="tpu_custom_call" | custom-call | tf_op jit(solution)/shard_map/pallas_call | solution.py:554
  66.3 1.7 %shard_map.68 = (f32[16,768]{1,0:T(8,128)}, f32[16,768]{1,0:T(8,128)}, f32[1,16]{1,0:T(1,128)}) custom-call(f32[16,1664]{1,0:T(8,128)} %shard_map.67.sums_ref, f32[16,768]{1,0:T(8,128)} %mean_ref.3, f32[16,768]{1,0:T(8,128)} %var_ref.3, f32[1,16]{1,0:T(1,128)} %bitcast.3), custom_call_target="tpu_custom_call" | custom-call | tf_op jit(solution)/shard_map/pallas_call | solution.py:580

commit v5 on v4

--- a/solution.py
+++ b/solution.py
@@ -172,6 +172,9 @@
     around(1, 1, A)
     around(-1, 1, B)
     across(0, 0)
+    around(1, 1, B)
+    around(-1, 1, A)
+    across(0, 1)
 
     emb_copy.wait()
 
@@ -187,9 +190,6 @@
         return carry
 
     lax.fori_loop(0, tiles // 2, prepare, 0)
-    around(1, 1, B)
-    around(-1, 1, A)
-    across(0, 1)
     lax.fori_loop(tiles // 2, tiles, prepare, 0)
 
     groups = ((0, -1, 1), (-2, 2), (-3, 3, 4))
@@ -318,33 +318,38 @@
         )
 
     def stat_start(h):
-        def body(t, carry):
+        for t in range(1, n_comp):
             stat_copy(h, t).start()
-            return carry
-
-        lax.fori_loop(1, n_comp, body, 0)
-
-    def responsibilities(h, counts):
-        def body(t, carry):
+
+    def factors(h):
+        for t in range(1, n_comp):
             stat_copy(h, t).wait_recv()
-            return carry
-
-        lax.fori_loop(1, n_comp, body, 0)
         logs = stats[h]
         peak = jnp.max(logs, axis=0)
         total = jnp.sum(jnp.exp(logs - peak[None]), axis=0)
         mine = slice(h * tiles // 2, (h + 1) * tiles // 2)
         fac[mine, :] = jnp.exp(fac[mine, :] - peak) / total
+
+    def responsibilities(h, g):
+        n, base = 2 * chunk * len(groups[g]), bases[g]
+        counts = mbuf[base : base + n, 2 * width :] if h else None
         for i in range(h * tiles // 2, (h + 1) * tiles // 2):
             lanes = slice(i * 128, (i + 1) * 128)
-            resp = st[:, lanes] * fac[i : i + 1, :]
+            resp = st[base : base + n, lanes] * fac[i : i + 1, :]
             counts = resp if counts is None else counts + resp
             hi, lo = split(resp)
-            for g, base in zip(groups, bases):
-                n = 2 * chunk * len(g)
-                rt[2 * base : 2 * base + n, lanes] = hi[base : base + n]
-                rt[2 * base + n : 2 * base + 2 * n, lanes] = lo[base : base + n]
-        return counts
+            rt[2 * base : 2 * base + n, lanes] = hi
+            rt[2 * base + n : 2 * base + 2 * n, lanes] = lo
+        mbuf[base : base + n, 2 * width :] = counts
+
+    def fold_counts(g):
+        n, base = 2 * chunk * len(groups[g]), bases[g]
+        counts = mbuf[base : base + n, 2 * width :]
+        counts = counts + pltpu.roll(counts, 64, 1)
+        for i in range(0, n, own):
+            mbuf[base + i + part : base + i + own, 2 * width :] = jnp.where(
+                low_lanes, counts[i : i + part], counts[i + part : i + own]
+            )
 
     score(2, 0, rows // 2, rows // 2)
     statistic(0)
@@ -461,18 +466,19 @@
             value += here[...]
         return value
 
-    counts = responsibilities(0, None)
+    factors(0)
+    responsibilities(0, 2)
     for i in range(2):
         moments(2, slice(i * width, (i + 1) * width), slice(0, rows // 2))
-    counts = responsibilities(1, counts)
-    counts = counts + pltpu.roll(counts, 64, 1)
-    mbuf[:, 2 * width :] = counts
-    for i in range(0, n_z * 2 * chunk, own):
-        mbuf[i + part : i + own, 2 * width :] = jnp.where(
-            low_lanes, counts[i : i + part], counts[i + part : i + own]
-        )
+    responsibilities(0, 1)
+    responsibilities(0, 0)
+    factors(1)
+    responsibilities(1, 2)
     moments_half(2, 0)
+    fold_counts(2)
     moments_half(2, 1)
+    responsibilities(1, 1)
+    fold_counts(1)
     moments_half(1, 0)
     add_sibling(2)
     give(4, 0)
@@ -486,6 +492,8 @@
     begin(-1, 2, A)
     begin(1, 2, A)
     begin(-1, 2, B)
+    responsibilities(1, 0)
+    fold_counts(0)
     moments_half(0, 0)
     add_sibling(1)
     merge(1)

time: 68.3 us -> 67.5 us (0.988)
  Pallas kernels: 67.5 us -> 66.5 us
    pallas_call x1, Pallas kernels: 65.7 us -> 64.7 us  [per_device(): pl.pallas_call(functools.partial(kernel, n_z, n_comp), out_shape=jax.Shap...]
where the time goes in v5:
time: 67.5 us; the launch traced here: 67.1 us
  Pallas kernels  66.5 us (99%)
    pallas_call x1, Pallas kernels, per_device(): pl.pallas_call(functools.partial(kernel, n_z, n_comp), out_shape=jax.Shap...  64.7 us
    pallas_call x1, Pallas kernels, per_device(): pl.pallas_call(functools.partial(update, group * n_comp / (rows * n_dp)),...  1.74 us

profile of v5, /device:TPU:1, one launch (start us, length us, event | category | flops | bytes accessed | tf_op | source)
XLA Modules:
  0.0 67.1 jit_solution(8505377194416284731)
XLA Ops:
  0.6 64.7 %shard_map.67.sums_ref = f32[16,1664]{1,0:T(8,128)} custom-call(f32[1024,768]{1,0:T(8,128)} %emb_hbm.1, f32[16,768]{1,0:T(8,128)} %mean_ref.3, f32[16,768]{1,0:T(8,128)} %var_ref.3, f32[1,16]{1,0:T(1,128)} %bitcast.2), custom_call_target="tpu_custom_call" | custom-call | tf_op jit(solution)/shard_map/pallas_call | solution.py:562
  65.4 1.7 %shard_map.68 = (f32[16,768]{1,0:T(8,128)}, f32[16,768]{1,0:T(8,128)}, f32[1,16]{1,0:T(1,128)}) custom-call(f32[16,1664]{1,0:T(8,128)} %shard_map.67.sums_ref, f32[16,768]{1,0:T(8,128)} %mean_ref.3, f32[16,768]{1,0:T(8,128)} %var_ref.3, f32[1,16]{1,0:T(1,128)} %bitcast.3), custom_call_target="tpu_custom_call" | custom-call | tf_op jit(solution)/shard_map/pallas_call | solution.py:588

commit v6 on v5

--- a/solution.py
+++ b/solution.py
@@ -479,7 +479,6 @@
     moments_half(2, 1)
     responsibilities(1, 1)
     fold_counts(1)
-    moments_half(1, 0)
     add_sibling(2)
     give(4, 0)
     give(4, 1)
@@ -487,6 +486,7 @@
     begin(-1, 2, S)
     begin(1, 2, Q)
     begin(-1, 2, Q)
+    moments_half(1, 0)
     moments_half(1, 1)
     begin(1, 2, B)
     begin(-1, 2, A)
@@ -500,12 +500,12 @@
     give(2, 1)
     merge(-1)
     give(-2, 1)
+    extend(1, 3, Q)
+    extend(-1, 3, Q)
     take(4, 0)
     begin(1, 1, A)
     take(4, 1)
     begin(-1, 1, B)
-    extend(1, 3, Q)
-    extend(-1, 3, Q)
     moments_half(0, 1)
     extend(-1, 3, A)
     add_sibling(0)

time: 67.5 us -> 67.5 us (level)
  no operation moved by 1% of the time
where the time goes in v6:
time: 67.5 us; the launch traced here: 67.3 us
  Pallas kernels  66.6 us (99%)
    pallas_call x1, Pallas kernels, per_device(): pl.pallas_call(functools.partial(kernel, n_z, n_comp), out_shape=jax.Shap...  64.9 us
    pallas_call x1, Pallas kernels, per_device(): pl.pallas_call(functools.partial(update, group * n_comp / (rows * n_dp)),...  1.74 us

profile of v6, /device:TPU:1, one launch (start us, length us, event | category | flops | bytes accessed | tf_op | source)
XLA Modules:
  0.0 67.3 jit_solution(2654711457779883484)
XLA Ops:
  0.6 64.9 %shard_map.67.sums_ref = f32[16,1664]{1,0:T(8,128)} custom-call(f32[1024,768]{1,0:T(8,128)} %emb_hbm.1, f32[16,768]{1,0:T(8,128)} %mean_ref.3, f32[16,768]{1,0:T(8,128)} %var_ref.3, f32[1,16]{1,0:T(1,128)} %bitcast.2), custom_call_target="tpu_custom_call" | custom-call | tf_op jit(solution)/shard_map/pallas_call | solution.py:562
  65.5 1.7 %shard_map.68 = (f32[16,768]{1,0:T(8,128)}, f32[16,768]{1,0:T(8,128)}, f32[1,16]{1,0:T(1,128)}) custom-call(f32[16,1664]{1,0:T(8,128)} %shard_map.67.sums_ref, f32[16,768]{1,0:T(8,128)} %mean_ref.3, f32[16,768]{1,0:T(8,128)} %var_ref.3, f32[1,16]{1,0:T(1,128)} %bitcast.3), custom_call_target="tpu_custom_call" | custom-call | tf_op jit(solution)/shard_map/pallas_call | solution.py:588
